TPU v7x, 128 devices: a whole 4x4x4 slice. The times are simulated.
128 devices in a mesh: samp: 16 (over z_lo, y, core), tp: 8 (over x, z_hi).
Axes of the slice: x: 4, y: 4, z: 4 (z_hi: 2, z_lo: 2; z = z_hi * 2 + z_lo), core: 2. Of those that a mesh axis runs over, the one named last changes fastest.
Arguments:
- prompt_rows: bfloat16 [32, 1536, 8, 2304], P('samp', None, 'tp'), may hold values from -6 to 6
- prompt_dt: bfloat16 [32, 1536, 8, 16], P('samp', None, 'tp'), may hold values from -3 to 3
- decode_rows: bfloat16 [32, 16, 2, 8, 2304], P(None, 'samp', None, 'tp'), may hold values from -6 to 6
- decode_dt: bfloat16 [32, 16, 2, 8, 16], P(None, 'samp', None, 'tp'), may hold values from -3 to 3
- placement: int32 [32], replicated, may hold values from 0 to 31, each once
- conv_weight: float32 [8, 4, 1280], P('tp'), may hold values from -3 to 3
- conv_bias: float32 [8, 1280], P('tp'), may hold values from -3 to 3
- dt_bias: float32 [8, 16], P('tp'), may hold values from -3 to -1.5
- a_log: float32 [8, 16], P('tp'), may hold values from -7.5 to -0.5
- skip_gain: float32 [8, 16], P('tp'), may hold values from -4 to 4
- norm_gain: float32 [8, 1024], P('tp'), may hold values from 0.1 to 1.9
Outputs:
- prefill_out: bfloat16 [32, 1536, 8, 1024], P('samp', 'tp')
- decode_out: bfloat16 [32, 16, 2, 8, 1024], P(None, 'samp', None, 'tp')
Inputs may be any that keep to these rules, and one draw needn't show every extreme that they name: `placement`: every slot appears once.
All inputs are finite; a program needn't handle non-finite values.
Results may differ from a plain program's by a relative error of at most 0.001.
Values may be sent and summed in bfloat16 or wider, within the bound.
A program may use at most 192 MiB of HBM per device.

v0:
```python
import functools

import jax
import jax.numpy as jnp
from jax import lax
from jax.experimental import pallas as pl
from jax.experimental.pallas import tpu as pltpu
from jax.sharding import PartitionSpec as P

MESH = pl.DeviceIdType.MESH
HIGHEST = lax.Precision.HIGHEST
F32 = jnp.float32
BF16 = jnp.bfloat16
EPS = 1e-05

HEADS = 16
HEAD = 64
INNER = HEADS * HEAD
STATE = 128
XBC = INNER + 2 * STATE
ROW = XBC + INNER
SPAN = 128
HALF = SPAN // 2
TP = 8


def split(value):
    high = value.astype(BF16)
    return high, (value - high.astype(F32)).astype(BF16)


def silu_of_half(half):
    return half + half * jnp.tanh(half)


def softplus(value):
    return jnp.maximum(value, 0.0) + jnp.log1p(jnp.exp(-jnp.abs(value)))


def dot(left, right, precision=None):
    return jnp.dot(left, right, preferred_element_type=F32, precision=precision)


def dot_first(left, right):
    return lax.dot_general(left, right, (((0,), (0,)), ((), ())), preferred_element_type=F32)


def dot_last(left, right, precision=None):
    return lax.dot_general(
        left, right, (((1,), (1,)), ((), ())), preferred_element_type=F32, precision=precision
    )


def iota(shape, axis):
    return lax.broadcasted_iota(jnp.int32, shape, axis)


def kernel(
    ns,
    length,
    rows_hbm,
    raw_dt,
    drows,
    ddt,
    placement,
    conv_w,
    conv_b,
    dt_bias,
    a_log,
    skip_gain,
    norm_gain,
    final,
    dec_out,
    gathered,
    rows,
    carry,
    xs,
    mats,
    bcs,
    fac_in,
    fac_out,
    ends,
    expand,
    fx,
    gated,
    state,
    halfw,
    skip,
    perm,
    perm2,
    perm3,
    dpieces,
    dsend,
    drecv,
    dtable,
    osend,
    orecv,
    in_sem,
    send_sem,
    recv_sem,
    own_sem,
    dsend_sem,
    drecv_sem,
    osend_sem,
    orecv_sem,
):
    me = lax.axis_index("tp")
    sm = lax.axis_index("samp")
    x0 = me // 2
    chunks = length // SPAN
    n256 = 16 * ns

    def rows_in(p, c):
        part = pl.ds(pl.multiple_of(c * SPAN, SPAN), SPAN)
        return pltpu.make_async_copy(rows_hbm.at[p, part], rows.at[p, part], in_sem.at[p, c])

    for p in range(2):
        lax.fori_loop(0, chunks, lambda c, _: (rows_in(p, c).start(), 0)[1], 0)

    barrier = pltpu.get_barrier_semaphore()
    for d in range(1, TP):
        pl.semaphore_signal(
            barrier, inc=1, device_id={"tp": lax.rem(me + d, TP)}, device_id_type=MESH
        )
    for d in range(1, ns):
        pl.semaphore_signal(
            barrier, inc=1, device_id={"samp": lax.rem(sm + d, ns)}, device_id_type=MESH
        )

    halfw[0:4, :] = conv_w[...] * 0.5
    halfw[4:5, :] = conv_b[...] * 0.5
    eye = iota((HEADS, HEADS), 0) == iota((HEADS, HEADS), 1)

    def column(row):
        return jnp.sum(jnp.where(eye, row, 0.0), axis=1, keepdims=True)

    bias_row = dt_bias[...]
    rate_row = -jnp.exp(a_log[...])
    bias_col = column(bias_row)
    rate_col = column(rate_row)
    own = (iota((HEADS, INNER), 0) == iota((HEADS, INNER), 1) // HEAD).astype(F32)
    expand[0:HEADS, :] = own.astype(BF16)
    expand[HEADS : 2 * HEADS, :] = own.astype(BF16)
    skip[...] = jnp.sum(own * column(skip_gain[...]), axis=0, keepdims=True)

    def prepare(p):
        upper = (iota((SPAN, SPAN), 0) <= iota((SPAN, SPAN), 1)).astype(F32)
        step = softplus(raw_dt[p].astype(F32) + bias_col)
        steps = jnp.concatenate([step[:, c * SPAN : (c + 1) * SPAN] for c in range(chunks)], axis=0)
        decay = steps * jnp.concatenate([rate_col] * chunks, axis=0)
        total = dot(decay, upper, HIGHEST)
        middle = 0.5 * total[:, SPAN - 1 : SPAN]
        from_middle = total - middle
        in_high, in_low = split(jnp.exp(-from_middle) * steps)
        out_high, out_low = split(jnp.exp(from_middle))
        for c in range(chunks):
            part = slice(c * HEADS, (c + 1) * HEADS)
            fac_in[c, 0:HEADS, :] = in_high[part]
            fac_in[c, HEADS : 2 * HEADS, :] = in_low[part]
            fac_out[c, 0:HEADS, :] = out_high[part]
            fac_out[c, HEADS : 2 * HEADS, :] = out_low[part]
            ends[c] = jnp.broadcast_to(
                jnp.sum(own * jnp.exp(middle[part]), axis=0, keepdims=True), (8, INNER)
            )

    n64 = 4 * ns
    n32 = 2 * ns

    def block_of(k):
        return pl.ds(pl.multiple_of(16 * k, 16), 16)

    def to_holder(d):
        peer = lax.rem(sm + d, ns)
        return pltpu.make_async_remote_copy(
            src_ref=dsend.at[block_of(peer)],
            dst_ref=drecv.at[block_of(sm)],
            send_sem=dsend_sem,
            recv_sem=drecv_sem,
            device_id={"samp": peer},
            device_id_type=MESH,
        )

    def sort_decode_rows():
        lanes = iota((1, n256), 1)
        slot_of = jnp.zeros((1, n256), jnp.int32)
        for prompt in range(n32):
            slot_of = jnp.where(lanes % n32 == prompt, placement[prompt], slot_of)
        r = iota((n256, n256), 0)
        s = iota((n256, n256), 1)
        perm[...] = jnp.where(
            ((r // 4) % 4 == s // n64)
            & (slot_of == 2 * (r // 16) + (r // 2) % 2)
            & (r % 2 == (s // n32) % 2),
            1.0,
            0.0,
        ).astype(BF16)
        perm2[...] = jnp.where(
            (r // n64 == (s // 4) % 4) & ((r // ns) % 4 == s % 4) & (r % ns == s // 16), 1.0, 0.0
        ).astype(BF16)
        r = iota((256, 256), 0)
        s = iota((256, 256), 1)
        perm3[...] = jnp.where((r % TP == s // 32) & (r // TP == s % 32), 1.0, 0.0).astype(BF16)
        unit = jnp.where(iota((n32, n32), 0) == iota((n32, n32), 1), 1.0, 0.0).astype(BF16)
        dpieces[...] = jnp.zeros_like(dpieces)
        for i in range(2):
            for q in range(4):
                part = slice(q * n64 + i * n32, q * n64 + (i + 1) * n32)
                dpieces[part, 0:512] = drows[:, i, q * 512 : (q + 1) * 512]
                if q < 2:
                    dpieces[part, 512:640] = drows[:, i, 2048 + q * 128 : 2176 + q * 128]
                if q == 2:
                    dpieces[part, 512 : 512 + HEADS] = dot_last(unit, ddt[i]).astype(BF16)
        dsend[...] = dot(perm[...], dpieces[...]).astype(BF16)
        drecv[block_of(sm), :] = dsend[block_of(sm), :]

    def conv_half(now, last, columns):
        both = jnp.concatenate([last, now], axis=0)
        result = halfw[4:5, columns] + halfw[3:4, columns] * now
        for back in range(1, 4):
            result = result + halfw[3 - back : 4 - back, columns] * pltpu.roll(both, back, 0)[8:]
        return result

    def first_pass(p, c):
        rows_in(p, c).wait()
        base = pl.multiple_of(c * SPAN, SPAN)
        part = pl.ds(base, SPAN)
        keep = jnp.where(c > 0, 1.0, 0.0).astype(F32)
        fx[...] = dot_first(fac_in[c], expand[...])
        for b in range(XBC // 128):
            columns = slice(b * 128, (b + 1) * 128)
            now = rows[p, part, columns].astype(F32)
            last = carry[p, :, columns].astype(F32)[8:16] * keep
            value = silu_of_half(conv_half(now, last, columns))
            if b < INNER // 128:
                xs[part, columns] = value
                high, low = split(value * fx[:, columns])
                mats[c, 0:128, columns] = low
                mats[c, 128:256, columns] = high
            else:
                bcs[c, :, b * 128 - INNER : (b + 1) * 128 - INNER] = value
        carry[p] = rows[p, pl.ds(pl.multiple_of(base + SPAN - 16, 16), 16), 0:XBC]
        b_high, b_low = split(bcs[c, :, 0:128].T)
        b_twice = jnp.concatenate([b_high, b_high], axis=1)
        for b in range(INNER // 256):
            columns = slice(b * 256, (b + 1) * 256)
            end = ends[c, 0:1, columns]
            entering = state[p, :, columns] * end
            high, low = split(entering)
            mats[c, 256:384, columns] = high
            mats[c, 384:512, columns] = low
            added = dot(b_twice, mats[c, 0:256, columns]) + dot(b_low, mats[c, 128:256, columns])
            state[p, :, columns] = end * (added + entering)

    def second_pass(p, unit, third):
        c = 3 * unit + third
        base = pl.multiple_of(c * SPAN, SPAN)
        part = pl.ds(base, SPAN)
        fx[...] = dot_first(fac_out[c], expand[...])
        b_now = bcs[c, :, 0:128]
        c_now = bcs[c, :, 128:256]
        scores = dot_last(c_now, b_now, HIGHEST)
        scores = jnp.where(iota((SPAN, SPAN), 0) >= iota((SPAN, SPAN), 1), scores, 0.0)
        s_high, s_low = split(scores)
        c_high, c_low = split(c_now)
        left = jnp.concatenate([s_high, s_high, c_high, c_high], axis=1)
        left_low = jnp.concatenate([s_low, c_low], axis=1)
        squares = jnp.zeros((SPAN, 128), F32)
        for b in range(INNER // 256):
            columns = slice(b * 256, (b + 1) * 256)
            y = dot(left, mats[c, :, columns]) + dot(left_low, mats[c, 128:384, columns])
            y = fx[:, columns] * y + skip[:, columns] * xs[part, columns]
            z_half = 0.5 * rows[p, part, XBC + b * 256 : XBC + (b + 1) * 256].astype(F32)
            g = y * silu_of_half(z_half)
            gated[:, columns] = g
            squares = squares + g[:, 0:128] * g[:, 0:128] + g[:, 128:256] * g[:, 128:256]
        mean = jnp.sum(squares, axis=1, keepdims=True) * (1.0 / INNER)
        scale = lax.rsqrt(mean + EPS)
        for b in range(INNER // 128):
            columns = slice(b * 128, (b + 1) * 128)
            rows[p, part, columns] = (gated[:, columns] * scale * norm_gain[:, columns]).astype(BF16)
        for half in range(2):
            piece = 2 * third + half
            dest = 2 * unit + piece // 3
            rank = lax.rem(piece, 3)
            source = rows.at[p, pl.ds(pl.multiple_of(base + half * HALF, HALF), HALF), pl.ds(0, INNER)]
            target = gathered.at[me, p, pl.ds(pl.multiple_of(rank * HALF, HALF), HALF)]

            @pl.when(dest != me)
            def _():
                pltpu.make_async_remote_copy(
                    src_ref=source,
                    dst_ref=target,
                    send_sem=send_sem.at[dest],
                    recv_sem=recv_sem.at[p, rank],
                    device_id={"tp": dest},
                    device_id_type=MESH,
                ).start()

            @pl.when(dest == me)
            def _():
                pltpu.make_async_copy(source, target, own_sem).start()

    def decode():
        for d in range(1, ns):
            to_holder(d).wait_send()
        pltpu.make_async_copy(
            drecv.at[pl.ds(0, 16 * (ns - 1))], drecv.at[pl.ds(0, 16 * (ns - 1))], drecv_sem
        ).wait()
        dtable[...] = dot(perm2[...], drecv[...])
        pieces = []
        for j in range(2):
            tail = carry[j].astype(F32)
            window = [tail[13:14], tail[14:15], tail[15:16]]
            gates, steps = [], []
            for i in range(2):
                at = [slice(q * n64 + (2 * j + i) * ns, q * n64 + (2 * j + i + 1) * ns) for q in range(4)]
                window.append(
                    jnp.concatenate(
                        [dtable[at[0], 0:512], dtable[at[1], 0:512], dtable[at[2], 0:256]], axis=1
                    )
                )
                gates.append(
                    jnp.concatenate(
                        [
                            dtable[at[2], 256:512],
                            dtable[at[3], 0:512],
                            dtable[at[0], 512:640],
                            dtable[at[1], 512:640],
                        ],
                        axis=1,
                    )
                )
                steps.append(softplus(dtable[at[2], 512 : 512 + HEADS] + bias_row))
            convs = []
            for i in range(2):
                half = halfw[4:5, :]
                for tap in range(4):
                    half = half + halfw[tap : tap + 1, :] * window[i + tap]
                convs.append(silu_of_half(half))
            x = [v[:, 0:INNER] for v in convs]
            b = [v[:, INNER : INNER + STATE] for v in convs]
            cc = [v[:, INNER + STATE : XBC] for v in convs]
            from_state = dot(jnp.concatenate(cc, axis=0), state[j], HIGHEST)
            wide_dt = [dot(v, own, HIGHEST) for v in steps]
            wide_decay = [dot(jnp.exp(v * rate_row), own, HIGHEST) for v in steps]

            def over(i, k):
                return jnp.sum(b[i] * cc[k], axis=1, keepdims=True)

            first = wide_dt[0] * x[0]
            second = wide_dt[1] * x[1]
            y = [
                wide_decay[0] * from_state[0:ns] + first * over(0, 0) + skip[...] * x[0],
                wide_decay[1] * (wide_decay[0] * from_state[ns : 2 * ns] + first * over(0, 1))
                + second * over(1, 1)
                + skip[...] * x[1],
            ]
            for i in range(2):
                g = y[i] * silu_of_half(0.5 * gates[i])
                scale = lax.rsqrt(jnp.sum(g * g, axis=1, keepdims=True) * (1.0 / INNER) + EPS)
                pieces.append((g * scale * norm_gain[...]).astype(BF16))
        table = jnp.concatenate(
            [v[:, q * 256 : (q + 1) * 256] for q in range(4) for v in pieces], axis=0
        )
        osend[...] = dot_first(perm2[...], table).astype(BF16)

        for d in range(1, ns):
            to_sample(d).start()
        orecv[block_of(sm), :] = osend[block_of(sm), :]

    def to_sample(d):
        peer = lax.rem(sm + d, ns)
        return pltpu.make_async_remote_copy(
            src_ref=osend.at[block_of(peer)],
            dst_ref=orecv.at[block_of(sm)],
            send_sem=osend_sem,
            recv_sem=orecv_sem,
            device_id={"samp": peer},
            device_id_type=MESH,
        )

    state[...] = jnp.zeros_like(state)
    carry[...] = jnp.zeros_like(carry)
    prepare(0)
    lead = 4
    lax.fori_loop(0, lead, lambda c, _: (first_pass(0, c), 0)[1], 0)
    pl.semaphore_wait(barrier, TP - 1 + ns - 1)
    edge = (x0 == 0) | (x0 == 3)
    one = jnp.where(edge, 0, 2)
    two = jnp.where(lax.rem(x0, 2) == 0, 1, jnp.where(x0 == 1, 0, 2))
    low = jnp.minimum(one, two)
    high = jnp.maximum(one, two)

    def body(t, _):
        p = t // (2 * chunks)
        u = lax.rem(t, 2 * chunks)
        lone = (p == 0) & ((u == lead) | (u == 10))
        is_first = jnp.where(p == 0, u < chunks + 2, u < chunks) & jnp.logical_not(lone)

        @pl.when(t == 2 * chunks)
        def _():
            prepare(1)

        @pl.when(is_first)
        def _():
            first_pass(p, jnp.where(p == 0, u - 1 - jnp.where(u > 10, 1, 0), u))

        @pl.when(jnp.logical_not(is_first))
        def _():
            later = u - chunks - 2
            later = later + jnp.where(later >= low, 1, 0)
            later = later + jnp.where(later >= high, 1, 0)
            k = jnp.where(u == lead, one, jnp.where(u == 10, two, later))
            k = jnp.where(p == 0, k, u - chunks)
            lane = lax.rem(k, 4)
            unit = lax.rem(x0 + 1 + lane, 4)
            row = k // 4
            second_pass(p, unit, jnp.where(lax.rem(lane + p, 2) == 0, row, 2 - row))

        @pl.when(t == lead)
        def _():
            sort_decode_rows()
            for d in range(1, ns):
                to_holder(d).start()

        @pl.when(t == 3 * chunks - 1)
        def _():
            decode()

        return 0

    lax.fori_loop(lead, 4 * chunks, body, 0)

    def interleave(p, rank):
        pltpu.make_async_copy(
            gathered.at[pl.ds(0, TP - 1), p, pl.ds(rank * HALF, HALF)],
            gathered.at[pl.ds(0, TP - 1), p, pl.ds(rank * HALF, HALF)],
            recv_sem.at[p, rank],
        ).wait()
        for half in range(2):
            at = pl.multiple_of(rank * HALF + half * 32, 32)
            for b in range(INNER // 256):
                columns = slice(b * 256, (b + 1) * 256)
                stacked = jnp.concatenate(
                    [gathered[g, p, pl.ds(at, 32), columns] for g in range(TP)], axis=0
                )
                first = pl.multiple_of((p * (length // TP) + at) * TP, 256)
                final[pl.ds(first, 256), columns] = dot(perm3[...], stacked).astype(BF16)

    pltpu.make_async_copy(gathered.at[me], gathered.at[me], own_sem).wait()
    lax.fori_loop(0, 3, lambda i, _: (interleave(0, i), 0)[1], 0)

    pltpu.make_async_copy(
        osend.at[pl.ds(0, 16 * (ns - 1))], osend.at[pl.ds(0, 16 * (ns - 1))], osend_sem
    ).wait()
    pltpu.make_async_copy(
        orecv.at[pl.ds(0, 16 * (ns - 1))], orecv.at[pl.ds(0, 16 * (ns - 1))], orecv_sem
    ).wait()
    table = dot_first(perm[...], orecv[...]).astype(BF16)
    for q in range(4):
        for i in range(2):
            part = table[q * n64 + i * n32 : q * n64 + (i + 1) * n32]
            dec_out[:, i, q * 256 : (q + 1) * 256] = part

    turn = 2 - 2 * lax.rem(me, 2)
    lax.fori_loop(0, 3, lambda i, _: (interleave(1, lax.rem(i + turn, 3)), 0)[1], 0)
    for d in range(1, TP):
        peer = lax.rem(me + d, TP)
        pltpu.make_async_copy(gathered.at[peer], gathered.at[peer], send_sem.at[peer]).wait()


def per_device(
    ns,
    prompt_rows,
    prompt_dt,
    decode_rows,
    decode_dt,
    placement,
    conv_weight,
    conv_bias,
    dt_bias,
    a_log,
    skip_gain,
    norm_gain,
):
    length = prompt_rows.shape[1]
    chunks = length // SPAN
    n64, n256 = 4 * ns, 16 * ns
    vmem = pl.BlockSpec(memory_space=pltpu.VMEM)
    hbm = pl.BlockSpec(memory_space=pl.ANY)
    final, dec = pl.pallas_call(
        functools.partial(kernel, ns, length),
        out_shape=(
            pltpu.VMEM((2 * length, INNER), BF16),
            pltpu.VMEM((2 * ns, 2, INNER), BF16),
        ),
        in_specs=[hbm, vmem, vmem, vmem, pl.BlockSpec(memory_space=pltpu.SMEM)] + [vmem] * 6,
        out_specs=(vmem, vmem),
        scratch_shapes=[
            pltpu.VMEM((TP, 2, length // TP, INNER), BF16),
            pltpu.VMEM((2, length, ROW), BF16),
            pltpu.VMEM((2, 16, XBC), BF16),
            pltpu.VMEM((length, INNER), F32),
            pltpu.VMEM((chunks, 4 * SPAN, INNER), BF16),
            pltpu.VMEM((chunks, SPAN, 2 * STATE), F32),
            pltpu.VMEM((chunks, 2 * HEADS, SPAN), BF16),
            pltpu.VMEM((chunks, 2 * HEADS, SPAN), BF16),
            pltpu.VMEM((chunks, 8, INNER), F32),
            pltpu.VMEM((2 * HEADS, INNER), BF16),
            pltpu.VMEM((SPAN, INNER), F32),
            pltpu.VMEM((SPAN, INNER), F32),
            pltpu.VMEM((2, STATE, INNER), F32),
            pltpu.VMEM((8, XBC), F32),
            pltpu.VMEM((1, INNER), F32),
            pltpu.VMEM((n256, n256), BF16),
            pltpu.VMEM((n256, n256), BF16),
            pltpu.VMEM((256, 256), BF16),
            pltpu.VMEM((n256, 640), BF16),
            pltpu.VMEM((n256, 640), BF16),
            pltpu.VMEM((n256, 640), BF16),
            pltpu.VMEM((n256, 640), F32),
            pltpu.VMEM((n256, 256), BF16),
            pltpu.VMEM((n256, 256), BF16),
            pltpu.SemaphoreType.DMA((2, chunks)),
            pltpu.SemaphoreType.DMA((TP,)),
            pltpu.SemaphoreType.DMA((2, 3)),
            pltpu.SemaphoreType.DMA,
            pltpu.SemaphoreType.DMA,
            pltpu.SemaphoreType.DMA,
            pltpu.SemaphoreType.DMA,
            pltpu.SemaphoreType.DMA,
        ],
        compiler_params=pltpu.CompilerParams(
            collective_id=0, has_side_effects=True, vmem_limit_bytes=52 * 2**20
        ),
    )(
        prompt_rows[:, :, 0, :],
        prompt_dt[:, :, 0, :].transpose(0, 2, 1),
        decode_rows[:, 0, :, 0, :],
        decode_dt[:, 0, :, 0, :].transpose(1, 2, 0),
        placement,
        conv_weight[0],
        conv_bias,
        dt_bias,
        a_log,
        skip_gain,
        norm_gain,
    )
    prefill_out = final.reshape(2, length // TP, TP, INNER)
    return prefill_out, dec.reshape(2 * ns, 1, 2, 1, INNER)


def solution(mesh):
    in_specs = (
        P("samp", None, "tp", None),
        P("samp", None, "tp", None),
        P(None, "samp", None, "tp", None),
        P(None, "samp", None, "tp", None),
        P(),
        P("tp", None, None),
        P("tp", None),
        P("tp", None),
        P("tp", None),
        P("tp", None),
        P("tp", None),
    )
    out_specs = (P("samp", "tp", None, None), P(None, "samp", None, "tp", None))
    return jax.shard_map(
        functools.partial(per_device, mesh.shape["samp"]),
        mesh=mesh,
        in_specs=in_specs,
        out_specs=out_specs,
        check_vma=False,
    )
```

profile of v0, /device:TPU:7, one launch (start us, length us, event | category | flops | bytes accessed | tf_op | source)
XLA Modules:
  0.0 97.1 jit_solution(10303483434813541038)
XLA Ops:
  0.6 93.0 %shard_map.122 = (bf16[3072,1024]{1,0:T(8,128)(2,1)S(1)}, bf16[32,2,1024]{2,1,0:T(2,128)(2,1)S(1)}) custom-call(bf16[2,1536,2304]{2,1,0:T(8,128)(2,1)} %bitcast.15, bf16[2,16,1536]{2,1,0:T(8,128)(2,1)} %bitcast.17, bf16[32,2,2304]{2,1,0:T(2,128)(2,1)} %bitcast.16, bf16[2,16,32]{2,1,0:T(8,128)(2,1)} %bitcast.19, s32[32]{0:T(128)} %placement.1, ...), custom_call_target="tpu_custom_call" | custom-call | tf_op jit(solution)/shard_map/pallas_call | solution.py:491
  93.7 2.7 %copy.16 = bf16[2,192,8,1024]{3,2,1,0:T(8,128)(2,1)} copy(bf16[2,192,8,1024]{3,2,1,0:T(8,128)(2,1)S(1)} %bitcast.13) | data formatting | bytes 12582912
  96.4 0.7 copy.17
where the time goes:
time: 97.2 us; the launch traced here: 97.1 us
  Pallas kernels  93 us (96%)
  local copies, waits for them, and re-layouts  3.36 us (3%)
    pallas_call x1, Pallas kernels, per_device(): pl.pallas_call(functools.partial(kernel, ns, length), out_shape=(pltpu.VM...  93 us
    unnamed x2, local copies, waits for them, and re-layouts  3.36 us

commit v1 on v0

--- a/solution.py
+++ b/solution.py
@@ -180,6 +180,16 @@
             device_id_type=MESH,
         )
 
+    def order_tables():
+        r = iota((n256, n256), 0)
+        s = iota((n256, n256), 1)
+        perm2[...] = jnp.where(
+            (r // n64 == (s // 4) % 4) & ((r // ns) % 4 == s % 4) & (r % ns == s // 16), 1.0, 0.0
+        ).astype(BF16)
+        r = iota((256, 256), 0)
+        s = iota((256, 256), 1)
+        perm3[...] = jnp.where((r % TP == s // 32) & (r // TP == s % 32), 1.0, 0.0).astype(BF16)
+
     def sort_decode_rows():
         lanes = iota((1, n256), 1)
         slot_of = jnp.zeros((1, n256), jnp.int32)
@@ -194,12 +204,6 @@
             1.0,
             0.0,
         ).astype(BF16)
-        perm2[...] = jnp.where(
-            (r // n64 == (s // 4) % 4) & ((r // ns) % 4 == s % 4) & (r % ns == s // 16), 1.0, 0.0
-        ).astype(BF16)
-        r = iota((256, 256), 0)
-        s = iota((256, 256), 1)
-        perm3[...] = jnp.where((r % TP == s // 32) & (r // TP == s % 32), 1.0, 0.0).astype(BF16)
         unit = jnp.where(iota((n32, n32), 0) == iota((n32, n32), 1), 1.0, 0.0).astype(BF16)
         dpieces[...] = jnp.zeros_like(dpieces)
         for i in range(2):
@@ -400,6 +404,7 @@
         @pl.when(t == 2 * chunks)
         def _():
             prepare(1)
+            order_tables()
 
         @pl.when(is_first)
         def _():

time: 97.2 us -> 97.1 us (level)
  no operation moved by 1% of the time
where the time goes in v1:
time: 97.1 us; the launch traced here: 97 us
  Pallas kernels  92.9 us (96%)
  local copies, waits for them, and re-layouts  3.36 us (3%)
    pallas_call x1, Pallas kernels, per_device(): pl.pallas_call(functools.partial(kernel, ns, length), out_shape=(pltpu.VM...  92.9 us
    unnamed x2, local copies, waits for them, and re-layouts  3.36 us

profile of v1, /device:TPU:7, one launch (start us, length us, event | category | flops | bytes accessed | tf_op | source)
XLA Modules:
  0.0 97.0 jit_solution(15884493081221856017)
XLA Ops:
  0.6 92.9 %shard_map.122 = (bf16[3072,1024]{1,0:T(8,128)(2,1)S(1)}, bf16[32,2,1024]{2,1,0:T(2,128)(2,1)S(1)}) custom-call(bf16[2,1536,2304]{2,1,0:T(8,128)(2,1)} %bitcast.15, bf16[2,16,1536]{2,1,0:T(8,128)(2,1)} %bitcast.17, bf16[32,2,2304]{2,1,0:T(2,128)(2,1)} %bitcast.16, bf16[2,16,32]{2,1,0:T(8,128)(2,1)} %bitcast.19, s32[32]{0:T(128)} %placement.1, ...), custom_call_target="tpu_custom_call" | custom-call | tf_op jit(solution)/shard_map/pallas_call | solution.py:496
  93.6 2.7 %copy.16 = bf16[2,192,8,1024]{3,2,1,0:T(8,128)(2,1)} copy(bf16[2,192,8,1024]{3,2,1,0:T(8,128)(2,1)S(1)} %bitcast.13) | data formatting | bytes 12582912
  96.3 0.7 copy.17
